TPU v7x, 128 devices: a whole 4x4x4 slice. The times are simulated.
128 devices in a mesh: seq: 16 (over x, z_hi, core), tp: 8 (over z_lo, y).
Axes of the slice: x: 4, y: 4, z: 4 (z_hi: 2, z_lo: 2; z = z_hi * 2 + z_lo), core: 2. Of those that a mesh axis runs over, the one named last changes fastest.
Arguments:
- query_stream: bfloat16 [4096, 8192], P('seq', 'tp'), may hold values from -6 to 6
- key_stream: bfloat16 [4096, 8192], P('seq', 'tp'), may hold values from -6 to 6
- value_stream: bfloat16 [4096, 8192], P('seq', 'tp'), may hold values from -6 to 6
- decay_rate: float32 [8192, 16], P('tp'), may hold values from 0.00012207031 to 0.08
- residue: float32 [8192, 16], P('tp'), may hold values from -2 to 2
- skip_gain: float32 [8192], P('tp'), may hold values from -3 to 3
- out_weight: bfloat16 [8192, 8192], P('seq', 'tp'), may hold values from -0.0625 to 0.0625
Outputs:
- mixed: bfloat16 [4096, 8192], P('seq', 'tp')
All inputs are finite; a program needn't handle non-finite values.
Results may differ from a plain program's by a relative error of at most 0.015.
Values may be sent and summed in bfloat16 or wider, within the bound.
A program may use at most 64 MiB of HBM per device.

v0:
```python
import math

import jax
import jax.numpy as jnp
from jax import lax
from jax.sharding import PartitionSpec as P

HIGH = lax.Precision.HIGHEST


def in_groups(func, arrays):
    count = arrays[0].shape[0]
    width = min(count, 64)
    shaped = tuple((a.reshape((count // width, width) + a.shape[1:]) for a in arrays))
    result = lax.map(lambda items: func(*items), shaped)
    return jax.tree.map(lambda r: r.reshape((count,) + r.shape[2:]), result)


def modal_conv(signal, rate, coef, start):
    width, length = signal.shape
    block_len = math.gcd(length, 128)
    nblock = length // block_len
    offsets = jnp.arange(block_len).astype(jnp.float32)
    decay = jnp.exp(-rate[:, :, None] * offsets[None, None, :])
    taps = jnp.einsum("gm,gmb->gb", coef, decay, precision=HIGH)
    lag = jnp.arange(block_len)[:, None] - jnp.arange(block_len)[None, :]
    toeplitz = jnp.where(lag[None, :, :] >= 0, taps[:, jnp.maximum(lag, 0)], 0.0)
    blocks = signal.reshape(width, nblock, block_len)
    inside = jnp.einsum("gij,gnj->gni", toeplitz, blocks, precision=HIGH)
    tails = decay[:, :, ::-1]
    ends = jnp.einsum("gnj,gmj->ngm", blocks, tails, precision=HIGH)
    power = jnp.exp(-rate * block_len)

    def advance(state, end_term):
        return (power * state + end_term, state)

    final, starts = lax.scan(advance, start, ends)
    lead = coef[:, :, None] * jnp.exp(-rate[:, :, None] * (offsets[None, None, :] + 1.0))
    inside = inside + jnp.einsum("ngm,gmi->gni", starts, lead, precision=HIGH)
    return (inside.reshape(width, length), final)


def body(query_stream, key_stream, value_stream, decay_rate, residue, skip_gain, out_weight):
    product = (key_stream.astype(jnp.float32) * value_stream.astype(jnp.float32)).astype(
        jnp.bfloat16
    )
    local_rows, local_chan = product.shape
    coef = residue * jnp.sqrt(-jnp.expm1(-2.0 * decay_rate))
    shards = lax.axis_size("seq")
    narrow = local_chan // shards
    whole = lax.all_to_all(product.T, "seq", split_axis=0, concat_axis=1, tiled=True)
    first = lax.axis_index("seq") * narrow
    rate_part = lax.dynamic_slice_in_dim(decay_rate, first, narrow, 0)
    coef_part = lax.dynamic_slice_in_dim(coef, first, narrow, 0)
    skip_part = lax.dynamic_slice_in_dim(skip_gain, first, narrow, 0)
    signal = whole.astype(jnp.float32)
    empty = jnp.zeros((narrow, decay_rate.shape[1]), jnp.float32)
    along, final = in_groups(modal_conv, (signal, rate_part, coef_part, empty))
    convolved = (along + skip_part[:, None] * signal).astype(jnp.bfloat16)
    convolved = lax.all_to_all(convolved, "seq", split_axis=1, concat_axis=0, tiled=True).T
    gated = (query_stream.astype(jnp.float32) * convolved.astype(jnp.float32)).astype(jnp.bfloat16)
    full_gated = lax.all_gather(gated, "tp", axis=1, tiled=True)
    mixed = jnp.dot(
        full_gated,
        lax.all_gather(out_weight, "seq", axis=0, tiled=True),
        preferred_element_type=jnp.float32,
    )
    return mixed.astype(jnp.bfloat16)


def solution(mesh):
    placed = (
        P("seq", "tp"),
        P("seq", "tp"),
        P("seq", "tp"),
        P("tp", None),
        P("tp", None),
        P("tp"),
        P("seq", "tp"),
    )
    return jax.shard_map(
        body, mesh=mesh, in_specs=placed, out_specs=P("seq", "tp"), check_vma=False
    )
```

profile of v0, /device:TPU:1, one launch (start us, length us, event | category | flops | bytes accessed | tf_op | source)
XLA Modules:
  0.0 297.1 jit_solution(15410088313621002754)
XLA Ops:
  6.5 1.2 copy.15
  7.8 1.2 copy.16
  9.0 0.9 multiply_convert_fusion
  10.0 9.1 %all-to-all-start = ((bf16[16,64,256]{2,1,0:T(8,128)(2,1)}), bf16[16,64,256]{2,1,0:T(8,128)(2,1)S(1)}, u32[]{:S(2)}, u32[]{:S(2)}) async-start(bf16[16,64,256]{2,1,0:T(8,128)(2,1)} %bitcast.1), calls=%async_computation | async-start | bytes 1048576 | tf_op jit(solution)/shard_map/all_to_all | solution.py:51
  19.1 0.8 multiply_exponential_fusion.1
  20.1 0.3 multiply_reduce_fusion
  20.8 54.4 %gather_fusion = f32[16384,64]{1,0:T(8,128)} fusion(f32[64,128]{0,1:T(8,128)S(1)} %copy.26, s32[16384]{0:T(1024)S(1)} %bitcast_clamp_fusion), kind=kCustom, calls=%fused_computation | custom fusion | bytes 8454144 | tf_op jit(solution)/shard_map/while/body/eval_jaxpr/gather | solution.py:27
  75.2 7.4 %copy.19 = f32[128,128,64]{1,0,2:T(8,128)} copy(f32[128,128,64]{2,1,0:T(8,128)} %bitcast.36) | data formatting | bytes 8388608 | tf_op jit(solution)/shard_map/while/body/eval_jaxpr/gather | solution.py:27
  82.6 0.8 dynamic_slice.25
  83.4 0.3 copy.17
  83.9 0.9 fusion.18
  84.8 0.3 copy.27
  85.1 1.6 while.20
  86.7 0.3 copy.21
  87.0 2.1 fusion.10
  89.1 5.1 %fusion.5 = f32[64,32,128]{2,1,0:T(8,128)S(1)} fusion(f32[64,32,128]{2,1,0:T(8,128)S(1)} %fusion.10, bf16[64,32,128]{2,1,0:T(8,128)(2,1)S(1)} %reshape.83, f32[128,128,64]{1,0,2:T(8,128)} %copy.19, pred[128,128]{1,0:T(8,128)(4,1)S(1)} %subtract_compare_fusion), kind=kOutput, calls=%fused_computation.8 | convolution fusion | flops 403963904 | bytes 6832128 | tf_op jit(solution)/shard_map/while/body/eval_jaxpr/gij,gnj->gni/dot_general | solution.py:29
  94.5 1.4 fusion.9
  96.0 7.2 %all-to-all-start.1 = ((bf16[64,16,256]{2,0,1:T(8,128)(2,1)}), bf16[64,16,256]{2,0,1:T(8,128)(2,1)S(1)}, u32[]{:S(2)}, u32[]{:S(2)}) async-start(bf16[64,16,256]{2,0,1:T(8,128)(2,1)} %fusion.9), calls=%async_computation.1 | async-start | bytes 1048576 | tf_op jit(solution)/shard_map/all_to_all | solution.py:60
  103.5 10.9 %all-to-all-done.1 = bf16[64,16,256]{2,0,1:T(8,128)(2,1)S(1)} async-done(((bf16[64,16,256]{2,0,1:T(8,128)(2,1)}), bf16[64,16,256]{2,0,1:T(8,128)(2,1)S(1)}, u32[]{:S(2)}, u32[]{:S(2)}) %all-to-all-start.1) | async-done | bytes 524320 | tf_op jit(solution)/shard_map/all_to_all | solution.py:60
  114.3 0.9 fusion.8
  115.5 0.5 all-gather.5.cloned.1.call-update
  116.0 50.1 %all-gather.3.cloned.1.call-done = bf16[256,8192]{0,1:T(8,128)(2,1)} async-done(((bf16[256,1024]{0,1:T(8,128)(2,1)}), bf16[256,8192]{0,1:T(8,128)(2,1)}) %all-gather.3.cloned.1.call-update) | async-done | bytes 4194320 | tf_op jit(solution)/shard_map/all_gather | solution.py:62
  166.1 111.8 %all-gather.5.cloned.1.call-done = bf16[8192,1024]{1,0:T(8,128)(2,1)} async-done(((bf16[512,1024]{1,0:T(8,128)(2,1)}), bf16[8192,1024]{1,0:T(8,128)(2,1)}) %all-gather.5.cloned.1.call-update) | async-done | bytes 16777232 | tf_op jit(solution)/shard_map/all_gather | solution.py:65
  277.9 12.4 %convolution_convert_fusion = bf16[256,1024]{1,0:T(8,128)(2,1)} fusion(bf16[256,8192]{0,1:T(8,128)(2,1)} %all-gather.3.cloned.1.call-done, bf16[8192,1024]{1,0:T(8,128)(2,1)} %all-gather.5.cloned.1.call-done), kind=kOutput, calls=%fused_computation.9 | convolution fusion | flops 4295229440 | bytes 21495808 | tf_op jit(solution)/shard_map/dot_general | solution.py:63
  (83 shorter events, 2.0 us)
Async XLA Ops:
  10.0 73.4 %all-to-all-start = ((bf16[16,64,256]{2,1,0:T(8,128)(2,1)}), bf16[16,64,256]{2,1,0:T(8,128)(2,1)S(1)}, u32[]{:S(2)}, u32[]{:S(2)}) async-start(bf16[16,64,256]{2,1,0:T(8,128)(2,1)} %bitcast.1), calls=%async_computation | async-start | bytes 1048576 | tf_op jit(solution)/shard_map/all_to_all | solution.py:51
  94.2 9.0 %copy-start = (bf16[256,1024]{1,0:T(8,128)(2,1)S(1)}, bf16[256,1024]{1,0:T(8,128)(2,1)}, u32[]{:S(2)}) copy-start(bf16[256,1024]{1,0:T(8,128)(2,1)} %param.9) | copy-start | bytes 1572868
  96.0 18.4 %all-to-all-start.1 = ((bf16[64,16,256]{2,0,1:T(8,128)(2,1)}), bf16[64,16,256]{2,0,1:T(8,128)(2,1)S(1)}, u32[]{:S(2)}, u32[]{:S(2)}) async-start(bf16[64,16,256]{2,0,1:T(8,128)(2,1)} %fusion.9), calls=%async_computation.1 | async-start | bytes 1048576 | tf_op jit(solution)/shard_map/all_to_all | solution.py:60
  103.2 62.9 %all-gather.3.cloned.1.call-start = ((), (), s32[]{:S(2)}) async-start(), calls=%async_computation.2 | async-start | bytes 4718592 | tf_op jit(solution)/shard_map/all_gather | solution.py:62
  115.3 162.6 %all-gather.5.cloned.1.call-start = ((), (), s32[]{:S(2)}) async-start(), calls=%async_computation.3 | async-start | bytes 17825792 | tf_op jit(solution)/shard_map/all_gather | solution.py:65
Sparse Core Ops, SparseCore 0:
  115.4 50.6 all-gather.2
  168.5 109.3 all-gather.4
where the time goes:
time: 298 us; the launch traced here: 297 us
  waiting for transfers between devices  173 us (58%)
  local copies, waits for them, and re-layouts  67.1 us (23%)
  matrix products  20.5 us (7%)
  starting transfers between devices  16.6 us (6%)
  between operations  13.6 us (5%)
  other arithmetic  5.04 us (2%)
    all_gather x1, waiting for transfers between devices, body(): lax.all_gather(out_weight, 'seq', axis=0, tiled=True)  112 us
    gather x2, local copies, waits for them, and re-layouts, modal_conv(): taps[:, jnp.maximum(lag, 0)]  61.8 us
    all_gather x1, waiting for transfers between devices, body(): full_gated = lax.all_gather(gated, 'tp', axis=1, tiled=True)  50.1 us
    dot_general x1, matrix products, body(): jnp.dot(full_gated, lax.all_gather(out_weight, 'seq', axis=0, tiled=True)...  12.4 us
    all_to_all x1, waiting for transfers between devices, body(): lax.all_to_all(convolved, 'seq', split_axis=1, concat_axis=0, tiled=True)  10.9 us
    all_to_all x1, starting transfers between devices, body(): lax.all_to_all(product.T, 'seq', split_axis=0, concat_axis=1, tiled=True)  9.13 us
    all_to_all x1, starting transfers between devices, body(): lax.all_to_all(convolved, 'seq', split_axis=1, concat_axis=0, tiled=True)  7.23 us
  transfers between devices with their start and end apart: 4, of which 3 were waited for; matrix products, arithmetic and copies ran while one was open for 22% of the time, Pallas kernels for 0%

commit v1 on v0

v1 whole, which is shorter than its diff:
```python
import functools

import jax
import jax.numpy as jnp
from jax import lax
from jax.experimental import pallas as pl
from jax.experimental.pallas import tpu as pltpu
from jax.sharding import PartitionSpec as P

MESH = pl.DeviceIdType.MESH
F32, BF16 = jnp.float32, jnp.bfloat16

ROWS, CHAN, KROWS, MODES = 256, 1024, 512, 16
SEG = ROWS // 8
LANES = 128
GROUPS = CHAN // LANES

PIECE = 64
NP = KROWS // PIECE
ZFIRST = 6
AHEAD = 2

X_RIGHT = (
    [(0, 0, p) for p in range(8)]
    + [(0, 1, 0), (-1, 0, 6)]
    + [(0, 1, p) for p in range(1, ZFIRST)]
    + [(-1, 0, p) for p in (0, 2, 4)]
    + [(-1, 1, p) for p in (0, 2, 4)]
)
X_LEFT = (
    [(0, 0, p) for p in range(8)]
    + [(0, 1, 0), (1, 0, 7)]
    + [(0, 1, p) for p in range(1, ZFIRST)]
    + [(1, 0, p) for p in (1, 3, 5)]
    + [(1, 1, p) for p in (1, 3, 5)]
)
Z_SEND = [(0, 0, p) for p in range(8)] + [None, None] + [(-1, 0, 6), (-1, 0, 7), (1, 0, 6), (1, 0, 7), (2, 0, 6), (2, 0, 7)]
NX, NZ = len(X_RIGHT), len(Z_SEND)

GP = 256
Y_RIGHT = [(0, 0, p) for p in range(4)] + [(0, 1, p) for p in range(4)] + [(-1, 0, 0), (-1, 0, 2), (-1, 1, 0), (-1, 1, 2)]
Y_LEFT = [(0, 0, p) for p in range(4)] + [(0, 1, p) for p in range(4)] + [(1, 0, 1), (1, 0, 3), (1, 1, 1), (1, 1, 3)]
NY = len(Y_RIGHT)


def expm1(u):
    series = jnp.ones_like(u)
    for n in range(8, 1, -1):
        series = 1.0 + series * u * (1.0 / n)
    return jnp.where(u > -0.3, u * series, jnp.exp(u) - 1.0)


def kernel(q_hbm, k_hbm, v_hbm, rate_hbm, res_hbm, skip_hbm, w_hbm, out_ref,
           q, k, v, rate, res, skip, wbuf, gbuf, acc, prod, conv, lam_b, coef_b, starts,
           e_own, e_sib, e_chip, e_in, s_in, lam_block,
           in_sem, own_sem, s_xr, r_xr, s_xl, r_xl, s_z, r_z, s_w, r_w, s_yr, r_yr, s_yl, r_yl, s_g, r_g,
           s_e, r_e, s_st, r_st):
    s, t = lax.axis_index("seq"), lax.axis_index("tp")
    x, zh, c = s // 4, (s // 2) % 2, s % 2
    zl, y = t // 4, t % 4
    j = s // 2

    def at(dx=0, dzh=0, dc=0, dy=0, dzl=0):
        x2, zh2, c2 = (x + dx + 4) % 4, (zh + dzh) % 2, (c + dc) % 2
        return ((x2 * 2 + zh2) * 2 + c2, ((zl + dzl) % 2) * 4 + (y + dy + 4) % 4)

    def chip_block(dx, dz):
        return ((x + dx + 4) % 4) * 2 + (zh + dz) % 2

    def remote(src, dst, ssem, rsem, device):
        return pltpu.make_async_remote_copy(
            src_ref=src, dst_ref=dst, send_sem=ssem, recv_sem=rsem, device_id=device, device_id_type=MESH
        )

    ins = [
        pltpu.make_async_copy(a, b, in_sem.at[i])
        for i, (a, b) in enumerate(
            ((k_hbm, k), (v_hbm, v), (rate_hbm, rate), (res_hbm, res), (skip_hbm, skip), (q_hbm, q))
        )
    ]
    for cp in ins:
        cp.start()
    partners = [at(dc=1), at(dy=1), at(dy=3), at(dzl=1)] + [
        at(dx=a, dzh=b) for a in range(4) for b in range(2) if (a, b) != (0, 0)
    ]
    barrier = pltpu.get_barrier_semaphore()
    for device in partners:
        pl.semaphore_signal(barrier, inc=1, device_id=device, device_id_type=MESH)

    for cp in ins:
        cp.wait()
    rate_t, res_t = rate[...].T, res[...].T
    lam_t = jnp.exp(-rate_t)
    coef_t = res_t * jnp.sqrt(-expm1(-2.0 * rate_t))
    for m in range(MODES):
        lam_b[m] = jnp.broadcast_to(lam_t[m : m + 1, :], (8, CHAN))
        coef_b[m] = jnp.broadcast_to(coef_t[m : m + 1, :], (8, CHAN))
    lam_block[...] = jnp.exp(-float(ROWS) * rate_t)
    pl.semaphore_wait(barrier, len(partners))

    sent = []

    def start(copy):
        copy.start()
        sent.append(copy)

    have = {(0, 0, p) for p in range(NP)}

    def piece(item):
        dx, dz, p = item
        return wbuf.at[chip_block(dx, dz) * 2 + c, pl.ds(p * PIECE, PIECE)]

    def source(item):
        dx, dz, p = item
        if (dx % 4, dz) == (0, 0):
            return w_hbm.at[pl.ds(p * PIECE, PIECE)]
        assert (dx % 4, dz, p) in have
        return piece(item)

    links = (
        (X_RIGHT, s_xr, r_xr, dict(dx=1), -1, 0),
        (X_LEFT, s_xl, r_xl, dict(dx=3), 1, 0),
        (Z_SEND, s_z, r_z, dict(dzh=1), 0, 1),
    )

    def issue(r):
        for items, ssem, rsem, where, _, _ in links:
            if r < len(items) and items[r] is not None:
                start(remote(source(items[r]), piece(items[r]), ssem.at[r], rsem.at[r], at(**where)))

    order = []

    def absorb(r):
        for items, ssem, rsem, where, ox, oz in links:
            if r < len(items) and items[r] is not None:
                dx, dz, p = items[r]
                item = ((dx + ox) % 4, (dz + oz) % 2, p)
                assert item not in have
                have.add(item)
                remote(piece(item), piece(item), ssem.at[r], rsem.at[r], at(**where)).wait_recv()
                n = len(order)
                order.append(item)
                start(remote(piece(item), piece(item), s_w.at[n], r_w.at[n], at(dc=1)))
        issue(r + AHEAD)

    def sibling_piece(item):
        dx, dz, p = item
        return wbuf.at[chip_block(dx, dz) * 2 + 1 - c, pl.ds(p * PIECE, PIECE)]

    taken = [0]

    def from_sibling(count):
        while taken[0] < count:
            n = taken[0]
            ref = sibling_piece(order[n])
            remote(ref, ref, s_w.at[n], r_w.at[n], at(dc=1)).wait_recv()
            taken[0] += 1

    for r in range(AHEAD):
        issue(r)
    own = wbuf.at[s]
    own_in = pltpu.make_async_copy(w_hbm, own, own_sem)
    own_in.start()
    start(remote(w_hbm, own, s_e.at[1], r_e.at[1], at(dc=1)))

    for g in range(GROUPS):
        lanes = pl.ds(g * LANES, LANES)
        prod[g] = (k[:, lanes].astype(F32) * v[:, lanes].astype(F32)).astype(BF16).astype(F32)
    seg_at = lax.broadcasted_iota(jnp.int32, (MODES, 8, LANES), 1)
    for g in range(GROUPS):
        lanes = pl.ds(g * LANES, LANES)
        lam = lam_b[:, :, lanes]

        def ends(i, state):
            return lam * state + prod[g, pl.ds(i, 8, stride=SEG), :][None]

        state = lax.fori_loop(0, SEG, ends, jnp.zeros((MODES, 8, LANES), F32), unroll=4)
        power = lam
        for _ in range(5):
            power = power * power
        scan = state
        for step in (1, 2, 4):
            moved = jnp.where(seg_at >= step, pltpu.roll(scan, step, 1), 0.0)
            scan = scan + power * moved
            power = power * power
        starts[:, :, lanes] = jnp.where(seg_at >= 1, pltpu.roll(scan, 1, 1), 0.0)
        for m in range(MODES):
            e_own[pl.ds(m, 1), lanes] = scan[m, 7:8, :]

    pass_e = remote(e_own, e_sib, s_e.at[0], r_e.at[0], at(dc=1))
    start(pass_e)
    pass_e.wait_recv()
    half = pl.ds(pl.multiple_of(8 * c, 8), 8)
    lam_h = lam_block[half, :]
    mine, other = e_own[half, :], e_sib[half, :]
    e_chip[...] = jnp.where(c == 0, lam_h * mine + other, lam_h * other + mine)
    later = []
    for d in range(1, 8):
        j2 = j + d
        device = ((j2 % 8) * 2 + c, t)
        later.append((j2 < 8, remote(e_chip, e_in.at[j], s_st.at[d], r_st.at[j], device)))
    for ok, copy in later:
        pl.when(ok)(copy.start)
    absorb(0)
    s_half = s_in.at[half, :]
    s_half[...] = jnp.zeros((8, CHAN), F32)
    lam2 = lam_h * lam_h
    for j1 in range(7):

        @pl.when(j1 < j)
        def _(j1=j1):
            remote(e_chip, e_in.at[j1], s_st.at[0], r_st.at[j1], at(dc=1)).wait_recv()
            s_half[...] = lam2 * s_half[...] + e_in[j1]

    pass_s = remote(s_half, s_half, s_e.at[2], r_e.at[2], at(dc=1))
    start(pass_s)
    pass_s_in = s_in.at[pl.ds(pl.multiple_of(8 - 8 * c, 8), 8), :]
    remote(pass_s_in, pass_s_in, s_e.at[2], r_e.at[2], at(dc=1)).wait_recv()
    absorb(1)

    have_g = set()

    def g_piece(item):
        dy, dz, p = item
        return gbuf.at[((zl + dz) % 2) * 4 + (y + dy + 4) % 4, :, pl.ds(p * GP, GP)]

    g_links = ((Y_RIGHT, s_yr, r_yr, dict(dy=1), -1), (Y_LEFT, s_yl, r_yl, dict(dy=3), 1))

    def issue_g(r):
        for items, ssem, rsem, where, _ in g_links:
            if r < NY:
                dy, dz, p = items[r]
                assert (dy % 4, dz, p) in have_g
                start(remote(g_piece(items[r]), g_piece(items[r]), ssem.at[r], rsem.at[r], at(**where)))

    def absorb_zl(p):
        ref = g_piece((0, 1, p))
        remote(ref, ref, s_g.at[p], r_g.at[p], at(dzl=1)).wait_recv()
        have_g.add((0, 1, p))

    def absorb_g(r):
        if r >= NY:
            return
        for items, ssem, rsem, where, oy in g_links:
            dy, dz, p = items[r]
            item = ((dy + oy) % 4, dz, p)
            ref = g_piece(item)
            remote(ref, ref, ssem.at[r], rsem.at[r], at(**where)).wait_recv()
            assert item not in have_g
            have_g.add(item)
        issue_g(r + AHEAD)

    before = jnp.where(c == 0, s_in[...], lam_block[...] * s_in[...] + e_sib[...])
    e_own_state = before
    row_seg = lax.broadcasted_iota(jnp.int32, (8, LANES), 0).astype(F32)
    for g in range(GROUPS):
        lanes = pl.ds(g * LANES, LANES)
        lam, coef = lam_b[:, :, lanes], coef_b[:, :, lanes]
        power = lam
        for _ in range(5):
            power = power * power
        lift = jnp.where(seg_at % 2 == 1, power, 1.0)
        power = power * power
        lift = lift * jnp.where((seg_at // 2) % 2 == 1, power, 1.0)
        power = power * power
        lift = lift * jnp.where(seg_at // 4 == 1, power, 1.0)
        first = jnp.stack([jnp.broadcast_to(e_own_state[m : m + 1, g * LANES : (g + 1) * LANES], (8, LANES)) for m in range(MODES)])
        gain = skip[:, lanes]

        def step(i, state):
            p = prod[g, pl.ds(i, 8, stride=SEG), :]
            state = lam * state + p[None]
            conv[g, pl.ds(i, 8, stride=SEG), :] = jnp.sum(coef * state, axis=0) + gain * p
            return state

        lax.fori_loop(0, SEG, step, starts[:, :, lanes] + lift * first, unroll=4)
        rounded = conv[g].astype(BF16).astype(F32)
        gbuf[t, :, lanes] = (q[:, lanes].astype(F32) * rounded).astype(BF16)
        if g % 2 == 1:
            p = g // 2
            have_g.add((0, 0, p))
            ref = g_piece((0, 0, p))
            start(remote(ref, ref, s_g.at[p], r_g.at[p], at(dzl=1)))
            if p < AHEAD:
                issue_g(p)
            if p == 1:
                absorb(2)

    g_base = 3
    for r in range(g_base, g_base + NY):
        rg = r - g_base
        absorb(r)
        if rg < 4:
            absorb_zl(rg)
        absorb_g(rg)
    at_round = g_base + NY

    own_in.wait()
    remote(w_hbm, wbuf.at[s + 1 - 2 * c], s_e.at[1], r_e.at[1], at(dc=1)).wait_recv()

    def multiply(dx, dz, first=False):
        b = chip_block(dx, dz)

        @pl.loop(0, CHAN, step=256)
        def _(n):
            cols = pl.ds(pl.multiple_of(n, 256), 256)
            w = wbuf[pl.ds(2 * b, 2), :, cols].reshape(2 * KROWS, 256)
            part = jnp.dot(gbuf[b], w, preferred_element_type=F32)
            acc[:, cols] = part if first else acc[:, cols] + part

    def complete(n):
        return sum(1 for item in order[:n])

    done = set()

    def ready():
        names = [(0, 0), (1, 0), (3, 0), (0, 1), (1, 1), (3, 1), (2, 0), (2, 1)]
        return [b for b in names if b not in done and all((*b, p) in have for p in range(NP))]

    def last_of(b):
        return max((i + 1 for i, item in enumerate(order) if item[:2] == b), default=0)

    for r in range(at_round, NX):
        todo = ready()[:2]
        for b in todo:
            from_sibling(last_of(b))
            multiply(*b, first=not done)
            done.add(b)
        absorb(r)
    for b in ready():
        from_sibling(last_of(b))
        multiply(*b, first=not done)
        done.add(b)
    from_sibling(len(order))
    assert len(done) == 8
    out_ref[...] = acc[...].astype(BF16)

    for copy in sent:
        copy.wait_send()
    for ok, copy in later:
        pl.when(ok)(copy.wait_send)


def body(query_stream, key_stream, value_stream, decay_rate, residue, skip_gain, out_weight):
    dma = pltpu.SemaphoreType.DMA
    n_w = 2 * NX + sum(i is not None for i in Z_SEND)
    vm = pltpu.VMEM
    return pl.pallas_call(
        kernel,
        out_shape=jax.ShapeDtypeStruct((ROWS, CHAN), BF16),
        in_specs=[pl.BlockSpec(memory_space=pl.ANY)] * 7,
        out_specs=pl.BlockSpec(memory_space=pltpu.VMEM),
        scratch_shapes=[
            vm((ROWS, CHAN), BF16), vm((ROWS, CHAN), BF16), vm((ROWS, CHAN), BF16),
            vm((CHAN, MODES), F32), vm((CHAN, MODES), F32), vm((1, CHAN), F32),
            vm((16, KROWS, CHAN), BF16), vm((8, ROWS, CHAN), BF16), vm((ROWS, CHAN), F32),
            vm((GROUPS, ROWS, LANES), F32), vm((GROUPS, ROWS, LANES), F32),
            vm((MODES, 8, CHAN), F32), vm((MODES, 8, CHAN), F32), vm((MODES, 8, CHAN), F32),
            vm((MODES, CHAN), F32), vm((MODES, CHAN), F32), vm((8, CHAN), F32), vm((7, 8, CHAN), F32),
            vm((MODES, CHAN), F32), vm((MODES, CHAN), F32),
            dma((6,)), dma, dma((NX,)), dma((NX,)), dma((NX,)), dma((NX,)), dma((NZ,)), dma((NZ,)),
            dma((n_w,)), dma((n_w,)), dma((NY,)), dma((NY,)), dma((NY,)), dma((NY,)), dma((4,)), dma((4,)),
            dma((3,)), dma((3,)), dma((8,)), dma((8,)),
        ],
        compiler_params=pltpu.CompilerParams(
            collective_id=0, has_side_effects=True, vmem_limit_bytes=56 << 20
        ),
        cost_estimate=pl.CostEstimate(flops=2 * ROWS * 8192 * CHAN, bytes_accessed=4 << 20, transcendentals=0),
        name="hyena",
    )(query_stream, key_stream, value_stream, decay_rate, residue, skip_gain[None], out_weight)


def solution(mesh):
    placed = (
        P("seq", "tp"),
        P("seq", "tp"),
        P("seq", "tp"),
        P("tp", None),
        P("tp", None),
        P("tp"),
        P("seq", "tp"),
    )
    return jax.shard_map(
        body, mesh=mesh, in_specs=placed, out_specs=P("seq", "tp"), check_vma=False
    )
```

time: 298 us -> 97.9 us (0.33)
  waiting for transfers between devices: 173 us -> 0 us
  Pallas kernels: 0 us -> 92.9 us
  local copies, waits for them, and re-layouts: 67.1 us -> 4.73 us
  matrix products: 20.5 us -> 0 us
  starting transfers between devices: 16.6 us -> 0 us
  between operations: 13.6 us -> 0.01 us
  other arithmetic: 5.04 us -> 0 us
    all_gather x2 -> x0, waiting for transfers between devices: 162 us -> none  [the longest x1 112 us: body(): lax.all_gather(out_weight, 'seq', axis=0, tiled=True)]
    pallas_call x0 -> x1, Pallas kernels: none -> 92.9 us  [body(): pl.pallas_call(kernel, out_shape=jax.ShapeDtypeStruct((ROWS, CHAN), BF16)...]
    gather x2 -> x0, local copies, waits for them, and re-layouts: 61.8 us -> none  [modal_conv(): taps[:, jnp.maximum(lag, 0)]]
    dot_general x4 -> x0, matrix products: 20.5 us -> none  [the longest x1 12.4 us: body(): jnp.dot(full_gated, lax.all_gather(out_weight, 'seq', axis=0, tiled=True)...]
    all_to_all x2 -> x0, starting transfers between devices: 16.4 us -> none  [the longest x1 9.13 us: body(): lax.all_to_all(product.T, 'seq', split_axis=0, concat_axis=1, tiled=True)]
    all_to_all x2 -> x0, waiting for transfers between devices: 10.9 us -> none  [the longest x1 10.9 us: body(): lax.all_to_all(convolved, 'seq', split_axis=1, concat_axis=0, tiled=True)]
    convert_element_type x4 -> x0, other arithmetic: 3.28 us -> none  [the longest x1 1.42 us: body(): convolved = (along + skip_part[:, None] * signal).astype(jnp.bfloat16)]
  transfers between devices with their start and end apart: 4 -> 0, of which waited for: 3 -> 0; matrix products, arithmetic and copies ran while one was open for 22% -> 0% of each run, Pallas kernels for 0% -> 0%
where the time goes in v1:
time: 97.9 us; the launch traced here: 97.6 us
  Pallas kernels  92.9 us (95%)
  local copies, waits for them, and re-layouts  4.73 us (5%)
    pallas_call x1, Pallas kernels, body(): pl.pallas_call(kernel, out_shape=jax.ShapeDtypeStruct((ROWS, CHAN), BF16)...  92.9 us
    unnamed x5, local copies, waits for them, and re-layouts  4.73 us

profile of v1, /device:TPU:1, one launch (start us, length us, event | category | flops | bytes accessed | tf_op | source)
XLA Modules:
  0.0 97.6 jit_solution(5002878961284163566)
XLA Ops:
  0.0 0.0 copy-start
  0.0 1.9 %copy.8.rate_hbm = f32[1024,16]{1,0:T(8,128)} copy(f32[1024,16]{0,1:T(8,128)} %param.10) | data formatting | bytes 131072 | tf_op args[3]
  1.9 0.0 copy-done
  1.9 1.0 %copy.9.res_hbm = f32[1024,16]{1,0:T(8,128)} copy(f32[1024,16]{0,1:T(8,128)S(1)} %copy-done) | data formatting | bytes 131072 | tf_op args[4]
  2.9 92.9 %hyena.1 = bf16[256,1024]{1,0:T(8,128)(2,1)} custom-call(bf16[256,1024]{1,0:T(8,128)(2,1)} %q_hbm.1, bf16[256,1024]{1,0:T(8,128)(2,1)} %k_hbm.1, bf16[256,1024]{1,0:T(8,128)(2,1)} %v_hbm.1, f32[1024,16]{1,0:T(8,128)} %copy.8.rate_hbm, f32[1024,16]{1,0:T(8,128)} %copy.9.res_hbm, f32[1,1024]{1,0:T(1,128)} %bitcast.1, bf16[512,1024]{1,0:T(8,128)(2,1)} %w_hbm.1), custom_call_target="tpu_custom_call" | custom-call | flops 4294967296 | bytes 4194304 | tf_op jit(solution)/shard_map/hyena/pallas_call | solution.py:348
  95.8 1.9 %copy.11 = bf16[256,1024]{1,0:T(8,128)(2,1)} copy(bf16[256,1024]{1,0:T(8,128)(2,1)} %hyena.1) | data formatting | bytes 1048576
Async XLA Ops:
  0.0 1.9 %copy-start = (f32[1024,16]{0,1:T(8,128)S(1)}, f32[1024,16]{0,1:T(8,128)}, u32[]{:S(2)}) copy-start(f32[1024,16]{0,1:T(8,128)} %param.11) | copy-start | bytes 196612

commit v2 on v1

--- a/solution.py
+++ b/solution.py
@@ -18,23 +18,30 @@
 PIECE = 64
 NP = KROWS // PIECE
 ZFIRST = 6
-AHEAD = 2
+EARLY = 2
+G_BASE = 5
 
 X_RIGHT = (
     [(0, 0, p) for p in range(8)]
-    + [(0, 1, 0), (-1, 0, 6)]
-    + [(0, 1, p) for p in range(1, ZFIRST)]
+    + [(0, 1, 0), (0, 1, 1), (0, 1, 2), (-1, 0, 6)]
+    + [(0, 1, p) for p in range(3, ZFIRST)]
     + [(-1, 0, p) for p in (0, 2, 4)]
     + [(-1, 1, p) for p in (0, 2, 4)]
 )
 X_LEFT = (
     [(0, 0, p) for p in range(8)]
-    + [(0, 1, 0), (1, 0, 7)]
-    + [(0, 1, p) for p in range(1, ZFIRST)]
+    + [(0, 1, 0), (0, 1, 1), (0, 1, 2), (1, 0, 7)]
+    + [(0, 1, p) for p in range(3, ZFIRST)]
     + [(1, 0, p) for p in (1, 3, 5)]
     + [(1, 1, p) for p in (1, 3, 5)]
 )
-Z_SEND = [(0, 0, p) for p in range(8)] + [None, None] + [(-1, 0, 6), (-1, 0, 7), (1, 0, 6), (1, 0, 7), (2, 0, 6), (2, 0, 7)]
+Z_EARLY = 5
+Z_SEND = (
+    [(0, 0, p) for p in range(Z_EARLY)]
+    + [None] * 4
+    + [(0, 0, p) for p in range(Z_EARLY, 8)]
+    + [(-1, 0, 6), (-1, 0, 7), (1, 0, 6), (1, 0, 7), (2, 0, 6), (2, 0, 7)]
+)
 NX, NZ = len(X_RIGHT), len(Z_SEND)
 
 GP = 256
@@ -53,7 +60,7 @@
 def kernel(q_hbm, k_hbm, v_hbm, rate_hbm, res_hbm, skip_hbm, w_hbm, out_ref,
            q, k, v, rate, res, skip, wbuf, gbuf, acc, prod, conv, lam_b, coef_b, starts,
            e_own, e_sib, e_chip, e_in, s_in, lam_block,
-           in_sem, own_sem, s_xr, r_xr, s_xl, r_xl, s_z, r_z, s_w, r_w, s_yr, r_yr, s_yl, r_yl, s_g, r_g,
+           in_sem, own_sem, r_xr, r_xl, r_z, s_w, r_w, r_yr, r_yl, s_g, r_g,
            s_e, r_e, s_st, r_st):
     s, t = lax.axis_index("seq"), lax.axis_index("tp")
     x, zh, c = s // 4, (s // 2) % 2, s % 2
@@ -87,81 +94,89 @@
     for device in partners:
         pl.semaphore_signal(barrier, inc=1, device_id=device, device_id_type=MESH)
 
+    pl.semaphore_wait(barrier, len(partners))
+
+    pieces_out = [0]
+    gated_out = [0]
+    sent = []
+
+    def start(copy):
+        copy.start()
+        sent.append(copy)
+
+    have = {(0, 0, p) for p in range(NP)}
+
+    def piece(item):
+        dx, dz, p = item
+        return wbuf.at[chip_block(dx, dz) * 2 + c, pl.ds(p * PIECE, PIECE)]
+
+    def source(item):
+        dx, dz, p = item
+        if (dx % 4, dz) == (0, 0):
+            return w_hbm.at[pl.ds(p * PIECE, PIECE)]
+        assert (dx % 4, dz, p) in have
+        return piece(item)
+
+    links = (
+        (X_RIGHT, r_xr, dict(dx=1), -1, 0),
+        (X_LEFT, r_xl, dict(dx=3), 1, 0),
+        (Z_SEND, r_z, dict(dzh=1), 0, 1),
+    )
+
+    issued = [0] * len(links)
+
+    limits = [EARLY, EARLY, EARLY]
+
+    def issue():
+        for i, (items, rsem, where, _, _) in enumerate(links):
+            while issued[i] < min(limits[i], len(items)):
+                r = issued[i]
+                if items[r] is not None:
+                    dx, dz, p = items[r]
+                    if (dx % 4, dz, p) not in have:
+                        break
+                    remote(source(items[r]), piece(items[r]), s_w, rsem.at[r], at(**where)).start()
+                    pieces_out[0] += 1
+                issued[i] += 1
+
+    def absorb(r):
+        for items, rsem, where, ox, oz in links:
+            if r < len(items) and items[r] is not None:
+                dx, dz, p = items[r]
+                item = ((dx + ox) % 4, (dz + oz) % 2, p)
+                assert item not in have
+                have.add(item)
+                ref = piece(item)
+                remote(ref, ref, s_w, rsem.at[r], at(**where)).wait_recv()
+                remote(ref, ref, s_w, r_w.at[group(item)], at(dc=1)).start()
+                pieces_out[0] += 1
+        issue()
+
+    def group(item):
+        dx, dz, p = item
+        return dx * 2 + dz + (4 if (dx, dz) == (2, 1) and p >= NP // 2 else 0)
+
+    def from_sibling(dx, dz, part=None):
+        rows = KROWS if part is None else KROWS // 2
+        first = (part or 0) * rows
+        ref = wbuf.at[chip_block(dx, dz) * 2 + 1 - c, pl.ds(first, rows)]
+        remote(ref, ref, s_w, r_w.at[group((dx, dz, first // PIECE))], at(dc=1)).wait_recv()
+
+    issue()
+    own = wbuf.at[s]
+    own_in = pltpu.make_async_copy(w_hbm, own, own_sem)
+    own_in.start()
+    start(remote(w_hbm, own, s_e.at[1], r_e.at[1], at(dc=1)))
+
     for cp in ins:
         cp.wait()
-    rate_t, res_t = rate[...].T, res[...].T
+    rate_t, res_t = rate[...], res[...]
     lam_t = jnp.exp(-rate_t)
     coef_t = res_t * jnp.sqrt(-expm1(-2.0 * rate_t))
     for m in range(MODES):
         lam_b[m] = jnp.broadcast_to(lam_t[m : m + 1, :], (8, CHAN))
         coef_b[m] = jnp.broadcast_to(coef_t[m : m + 1, :], (8, CHAN))
     lam_block[...] = jnp.exp(-float(ROWS) * rate_t)
-    pl.semaphore_wait(barrier, len(partners))
-
-    sent = []
-
-    def start(copy):
-        copy.start()
-        sent.append(copy)
-
-    have = {(0, 0, p) for p in range(NP)}
-
-    def piece(item):
-        dx, dz, p = item
-        return wbuf.at[chip_block(dx, dz) * 2 + c, pl.ds(p * PIECE, PIECE)]
-
-    def source(item):
-        dx, dz, p = item
-        if (dx % 4, dz) == (0, 0):
-            return w_hbm.at[pl.ds(p * PIECE, PIECE)]
-        assert (dx % 4, dz, p) in have
-        return piece(item)
-
-    links = (
-        (X_RIGHT, s_xr, r_xr, dict(dx=1), -1, 0),
-        (X_LEFT, s_xl, r_xl, dict(dx=3), 1, 0),
-        (Z_SEND, s_z, r_z, dict(dzh=1), 0, 1),
-    )
-
-    def issue(r):
-        for items, ssem, rsem, where, _, _ in links:
-            if r < len(items) and items[r] is not None:
-                start(remote(source(items[r]), piece(items[r]), ssem.at[r], rsem.at[r], at(**where)))
-
-    order = []
-
-    def absorb(r):
-        for items, ssem, rsem, where, ox, oz in links:
-            if r < len(items) and items[r] is not None:
-                dx, dz, p = items[r]
-                item = ((dx + ox) % 4, (dz + oz) % 2, p)
-                assert item not in have
-                have.add(item)
-                remote(piece(item), piece(item), ssem.at[r], rsem.at[r], at(**where)).wait_recv()
-                n = len(order)
-                order.append(item)
-                start(remote(piece(item), piece(item), s_w.at[n], r_w.at[n], at(dc=1)))
-        issue(r + AHEAD)
-
-    def sibling_piece(item):
-        dx, dz, p = item
-        return wbuf.at[chip_block(dx, dz) * 2 + 1 - c, pl.ds(p * PIECE, PIECE)]
-
-    taken = [0]
-
-    def from_sibling(count):
-        while taken[0] < count:
-            n = taken[0]
-            ref = sibling_piece(order[n])
-            remote(ref, ref, s_w.at[n], r_w.at[n], at(dc=1)).wait_recv()
-            taken[0] += 1
-
-    for r in range(AHEAD):
-        issue(r)
-    own = wbuf.at[s]
-    own_in = pltpu.make_async_copy(w_hbm, own, own_sem)
-    own_in.start()
-    start(remote(w_hbm, own, s_e.at[1], r_e.at[1], at(dc=1)))
 
     for g in range(GROUPS):
         lanes = pl.ds(g * LANES, LANES)
@@ -201,6 +216,7 @@
         later.append((j2 < 8, remote(e_chip, e_in.at[j], s_st.at[d], r_st.at[j], device)))
     for ok, copy in later:
         pl.when(ok)(copy.start)
+    limits[:] = [NX, NX, Z_EARLY]
     absorb(0)
     s_half = s_in.at[half, :]
     s_half[...] = jnp.zeros((8, CHAN), F32)
@@ -224,31 +240,39 @@
         dy, dz, p = item
         return gbuf.at[((zl + dz) % 2) * 4 + (y + dy + 4) % 4, :, pl.ds(p * GP, GP)]
 
-    g_links = ((Y_RIGHT, s_yr, r_yr, dict(dy=1), -1), (Y_LEFT, s_yl, r_yl, dict(dy=3), 1))
-
-    def issue_g(r):
-        for items, ssem, rsem, where, _ in g_links:
-            if r < NY:
+    g_links = ((Y_RIGHT, r_yr, dict(dy=1), -1), (Y_LEFT, r_yl, dict(dy=3), 1))
+
+    issued_g = [0] * len(g_links)
+
+    def issue_g():
+        for i, (items, rsem, where, _) in enumerate(g_links):
+            while issued_g[i] < NY:
+                r = issued_g[i]
                 dy, dz, p = items[r]
-                assert (dy % 4, dz, p) in have_g
-                start(remote(g_piece(items[r]), g_piece(items[r]), ssem.at[r], rsem.at[r], at(**where)))
+                if (dy % 4, dz, p) not in have_g:
+                    break
+                ref = g_piece(items[r])
+                remote(ref, ref, s_g, rsem.at[r], at(**where)).start()
+                gated_out[0] += 1
+                issued_g[i] += 1
 
     def absorb_zl(p):
         ref = g_piece((0, 1, p))
-        remote(ref, ref, s_g.at[p], r_g.at[p], at(dzl=1)).wait_recv()
+        remote(ref, ref, s_g, r_g.at[p], at(dzl=1)).wait_recv()
         have_g.add((0, 1, p))
+        issue_g()
 
     def absorb_g(r):
         if r >= NY:
             return
-        for items, ssem, rsem, where, oy in g_links:
+        for items, rsem, where, oy in g_links:
             dy, dz, p = items[r]
             item = ((dy + oy) % 4, dz, p)
             ref = g_piece(item)
-            remote(ref, ref, ssem.at[r], rsem.at[r], at(**where)).wait_recv()
+            remote(ref, ref, s_g, rsem.at[r], at(**where)).wait_recv()
             assert item not in have_g
             have_g.add(item)
-        issue_g(r + AHEAD)
+        issue_g()
 
     before = jnp.where(c == 0, s_in[...], lam_block[...] * s_in[...] + e_sib[...])
     e_own_state = before
@@ -280,70 +304,80 @@
             p = g // 2
             have_g.add((0, 0, p))
             ref = g_piece((0, 0, p))
-            start(remote(ref, ref, s_g.at[p], r_g.at[p], at(dzl=1)))
-            if p < AHEAD:
-                issue_g(p)
+            remote(ref, ref, s_g, r_g.at[p], at(dzl=1)).start()
+            gated_out[0] += 1
+            issue_g()
             if p == 1:
                 absorb(2)
 
-    g_base = 3
-    for r in range(g_base, g_base + NY):
-        rg = r - g_base
+    limits[2] = NZ
+    issue()
+    for r in range(3, G_BASE + NY):
         absorb(r)
-        if rg < 4:
+        rg = r - G_BASE
+        if 0 <= rg < 4:
             absorb_zl(rg)
-        absorb_g(rg)
-    at_round = g_base + NY
+        if 0 <= rg:
+            absorb_g(rg)
 
     own_in.wait()
     remote(w_hbm, wbuf.at[s + 1 - 2 * c], s_e.at[1], r_e.at[1], at(dc=1)).wait_recv()
 
-    def multiply(dx, dz, first=False):
+    def multiply(dx, dz, part=None, first=False):
         b = chip_block(dx, dz)
+        rows = KROWS if part is None else KROWS // 2
+        at_row = (part or 0) * rows
 
         @pl.loop(0, CHAN, step=256)
         def _(n):
             cols = pl.ds(pl.multiple_of(n, 256), 256)
-            w = wbuf[pl.ds(2 * b, 2), :, cols].reshape(2 * KROWS, 256)
-            part = jnp.dot(gbuf[b], w, preferred_element_type=F32)
-            acc[:, cols] = part if first else acc[:, cols] + part
-
-    def complete(n):
-        return sum(1 for item in order[:n])
+            if part is None:
+                w = wbuf[pl.ds(2 * b, 2), :, cols].reshape(2 * KROWS, 256)
+                total = jnp.dot(gbuf[b], w, preferred_element_type=F32)
+            else:
+                total = sum(
+                    jnp.dot(
+                        gbuf[b, :, pl.ds(h * KROWS + at_row, rows)],
+                        wbuf[2 * b + h, pl.ds(at_row, rows), cols],
+                        preferred_element_type=F32,
+                    )
+                    for h in range(2)
+                )
+            acc[:, cols] = total if first else acc[:, cols] + total
 
     done = set()
-
-    def ready():
-        names = [(0, 0), (1, 0), (3, 0), (0, 1), (1, 1), (3, 1), (2, 0), (2, 1)]
-        return [b for b in names if b not in done and all((*b, p) in have for p in range(NP))]
-
-    def last_of(b):
-        return max((i + 1 for i, item in enumerate(order) if item[:2] == b), default=0)
-
-    for r in range(at_round, NX):
-        todo = ready()[:2]
-        for b in todo:
-            from_sibling(last_of(b))
+    blocks = [(0, 0), (1, 0), (3, 0), (0, 1), (1, 1), (3, 1), (2, 0)]
+
+    def work(most):
+        for b in [b for b in blocks if b not in done and all((*b, p) in have for p in range(NP))][:most]:
+            if b != (0, 0):
+                from_sibling(*b)
             multiply(*b, first=not done)
             done.add(b)
+
+    for r in range(G_BASE + NY, NX):
+        work(2)
         absorb(r)
-    for b in ready():
-        from_sibling(last_of(b))
-        multiply(*b, first=not done)
-        done.add(b)
-    from_sibling(len(order))
-    assert len(done) == 8
+    work(8)
+    assert len(done) == 7
+    for part in range(2):
+        from_sibling(2, 1, part)
+        multiply(2, 1, part)
     out_ref[...] = acc[...].astype(BF16)
 
     for copy in sent:
         copy.wait_send()
+    assert pieces_out[0] * PIECE % KROWS == 0 and gated_out[0] % 4 == 0
+    ref = wbuf.at[pl.ds(0, pieces_out[0] * PIECE // KROWS)]
+    remote(ref, ref, s_w, r_w.at[0], at(dc=1)).wait_send()
+    ref = gbuf.at[pl.ds(0, gated_out[0] // 4)]
+    remote(ref, ref, s_g, r_g.at[0], at(dc=1)).wait_send()
     for ok, copy in later:
         pl.when(ok)(copy.wait_send)
 
 
 def body(query_stream, key_stream, value_stream, decay_rate, residue, skip_gain, out_weight):
     dma = pltpu.SemaphoreType.DMA
-    n_w = 2 * NX + sum(i is not None for i in Z_SEND)
     vm = pltpu.VMEM
     return pl.pallas_call(
         kernel,
@@ -352,14 +386,13 @@
         out_specs=pl.BlockSpec(memory_space=pltpu.VMEM),
         scratch_shapes=[
             vm((ROWS, CHAN), BF16), vm((ROWS, CHAN), BF16), vm((ROWS, CHAN), BF16),
-            vm((CHAN, MODES), F32), vm((CHAN, MODES), F32), vm((1, CHAN), F32),
+            vm((MODES, CHAN), F32), vm((MODES, CHAN), F32), vm((1, CHAN), F32),
             vm((16, KROWS, CHAN), BF16), vm((8, ROWS, CHAN), BF16), vm((ROWS, CHAN), F32),
             vm((GROUPS, ROWS, LANES), F32), vm((GROUPS, ROWS, LANES), F32),
             vm((MODES, 8, CHAN), F32), vm((MODES, 8, CHAN), F32), vm((MODES, 8, CHAN), F32),
             vm((MODES, CHAN), F32), vm((MODES, CHAN), F32), vm((8, CHAN), F32), vm((7, 8, CHAN), F32),
             vm((MODES, CHAN), F32), vm((MODES, CHAN), F32),
-            dma((6,)), dma, dma((NX,)), dma((NX,)), dma((NX,)), dma((NX,)), dma((NZ,)), dma((NZ,)),
-            dma((n_w,)), dma((n_w,)), dma((NY,)), dma((NY,)), dma((NY,)), dma((NY,)), dma((4,)), dma((4,)),
+            dma((6,)), dma, dma((NX,)), dma((NX,)), dma((NZ,)), dma, dma((10,)), dma((NY,)), dma((NY,)), dma, dma((4,)),
             dma((3,)), dma((3,)), dma((8,)), dma((8,)),
         ],
         compiler_params=pltpu.CompilerParams(
@@ -367,7 +400,7 @@
         ),
         cost_estimate=pl.CostEstimate(flops=2 * ROWS * 8192 * CHAN, bytes_accessed=4 << 20, transcendentals=0),
         name="hyena",
-    )(query_stream, key_stream, value_stream, decay_rate, residue, skip_gain[None], out_weight)
+    )(query_stream, key_stream, value_stream, decay_rate.T, residue.T, skip_gain[None], out_weight)
 
 
 def solution(mesh):

time: 97.9 us -> 76 us (0.78)
  Pallas kernels: 92.9 us -> 73.3 us
  local copies, waits for them, and re-layouts: 4.73 us -> 1.87 us
    pallas_call x1, Pallas kernels: 92.9 us -> 73.3 us  [body(): pl.pallas_call(kernel, out_shape=jax.ShapeDtypeStruct((ROWS, CHAN), BF16)...]
    unnamed x5 -> x1, local copies, waits for them, and re-layouts: 4.73 us -> 1.87 us
where the time goes in v2:
time: 76 us; the launch traced here: 75.2 us
  Pallas kernels  73.3 us (96%)
  local copies, waits for them, and re-layouts  1.87 us (2%)
    pallas_call x1, Pallas kernels, body(): pl.pallas_call(kernel, out_shape=jax.ShapeDtypeStruct((ROWS, CHAN), BF16)...  73.3 us
    unnamed x1, local copies, waits for them, and re-layouts  1.87 us

profile of v2, /device:TPU:1, one launch (start us, length us, event | category | flops | bytes accessed | tf_op | source)
XLA Modules:
  0.0 75.2 jit_solution(13658913312934389240)
XLA Ops:
  0.0 73.3 %hyena.1 = bf16[256,1024]{1,0:T(8,128)(2,1)} custom-call(bf16[256,1024]{1,0:T(8,128)(2,1)} %q_hbm.1, bf16[256,1024]{1,0:T(8,128)(2,1)} %k_hbm.1, bf16[256,1024]{1,0:T(8,128)(2,1)} %v_hbm.1, f32[16,1024]{1,0:T(8,128)} %bitcast.3, f32[16,1024]{1,0:T(8,128)} %bitcast.4, f32[1,1024]{1,0:T(1,128)} %bitcast.5, bf16[512,1024]{1,0:T(8,128)(2,1)} %w_hbm.1), custom_call_target="tpu_custom_call" | custom-call | flops 4294967296 | bytes 4194304 | tf_op jit(solution)/shard_map/hyena/pallas_call | solution.py:382
  73.3 1.9 %copy.9 = bf16[256,1024]{1,0:T(8,128)(2,1)} copy(bf16[256,1024]{1,0:T(8,128)(2,1)} %hyena.1) | data formatting | bytes 1048576

commit v3 on v2

--- a/solution.py
+++ b/solution.py
@@ -15,39 +15,51 @@
 LANES = 128
 GROUPS = CHAN // LANES
 
-PIECE = 64
-NP = KROWS // PIECE
-ZFIRST = 6
+PIECES = (64, 64, 64, 64, 64, 32, 32, 64, 64)
+STARTS = tuple(sum(PIECES[:p]) for p in range(len(PIECES)))
+NP, ZFIRST, HALF_P = len(PIECES), 6, 4
+UNIT = 64
+
 EARLY = 2
-G_BASE = 5
-
+Z_STATES = 3
+Z_EARLY = 5
+
+OWN = [(0, 0, p) for p in range(NP)]
 X_RIGHT = (
-    [(0, 0, p) for p in range(8)]
+    OWN
     + [(0, 1, 0), (0, 1, 1), (0, 1, 2), (-1, 0, 6)]
-    + [(0, 1, p) for p in range(3, ZFIRST)]
-    + [(-1, 0, p) for p in (0, 2, 4)]
-    + [(-1, 1, p) for p in (0, 2, 4)]
+    + [(0, 1, 3), (0, 1, 4), (0, 1, 5)]
+    + [(-1, 0, p) for p in (0, 2, 4, 5)]
+    + [(-1, 1, p) for p in (0, 2, 5)]
 )
 X_LEFT = (
-    [(0, 0, p) for p in range(8)]
-    + [(0, 1, 0), (0, 1, 1), (0, 1, 2), (1, 0, 7)]
-    + [(0, 1, p) for p in range(3, ZFIRST)]
-    + [(1, 0, p) for p in (1, 3, 5)]
-    + [(1, 1, p) for p in (1, 3, 5)]
+    OWN
+    + [(0, 1, 0), (0, 1, 1), (0, 1, 2), (1, 0, 7), (1, 0, 8)]
+    + [(0, 1, 3), (0, 1, 4), (0, 1, 5)]
+    + [(1, 0, p) for p in (1, 3)]
+    + [(1, 1, p) for p in (1, 3, 4)]
 )
-Z_EARLY = 5
 Z_SEND = (
-    [(0, 0, p) for p in range(Z_EARLY)]
+    OWN[:Z_EARLY]
     + [None] * 4
-    + [(0, 0, p) for p in range(Z_EARLY, 8)]
-    + [(-1, 0, 6), (-1, 0, 7), (1, 0, 6), (1, 0, 7), (2, 0, 6), (2, 0, 7)]
+    + OWN[Z_EARLY:]
+    + [(dx, 0, p) for dx in (-1, 1, 2) for p in (6, 7, 8)]
 )
-NX, NZ = len(X_RIGHT), len(Z_SEND)
+
+
+def times(items):
+    total, out = 0.0, []
+    for item in items:
+        total += 1.0 if item is None else PIECES[item[2]] / UNIT
+        out.append(total)
+    return out
+
 
 GP = 256
 Y_RIGHT = [(0, 0, p) for p in range(4)] + [(0, 1, p) for p in range(4)] + [(-1, 0, 0), (-1, 0, 2), (-1, 1, 0), (-1, 1, 2)]
 Y_LEFT = [(0, 0, p) for p in range(4)] + [(0, 1, p) for p in range(4)] + [(1, 0, 1), (1, 0, 3), (1, 1, 1), (1, 1, 3)]
 NY = len(Y_RIGHT)
+Y_AT = 5.3
 
 
 def expm1(u):
@@ -59,13 +71,12 @@
 
 def kernel(q_hbm, k_hbm, v_hbm, rate_hbm, res_hbm, skip_hbm, w_hbm, out_ref,
            q, k, v, rate, res, skip, wbuf, gbuf, acc, prod, conv, lam_b, coef_b, starts,
-           e_own, e_sib, e_chip, e_in, s_in, lam_block,
+           e_own, e_sib, e_chip, e_in, e_zh, a_own, a_zh, s_in, lam_block,
            in_sem, own_sem, r_xr, r_xl, r_z, s_w, r_w, r_yr, r_yl, s_g, r_g,
            s_e, r_e, s_st, r_st):
     s, t = lax.axis_index("seq"), lax.axis_index("tp")
     x, zh, c = s // 4, (s // 2) % 2, s % 2
     zl, y = t // 4, t % 4
-    j = s // 2
 
     def at(dx=0, dzh=0, dc=0, dy=0, dzl=0):
         x2, zh2, c2 = (x + dx + 4) % 4, (zh + dzh) % 2, (c + dc) % 2
@@ -88,7 +99,7 @@
     for cp in ins:
         cp.start()
     partners = [at(dc=1), at(dy=1), at(dy=3), at(dzl=1)] + [
-        at(dx=a, dzh=b) for a in range(4) for b in range(2) if (a, b) != (0, 0)
+        at(dx=1), at(dx=2), at(dx=3), at(dzh=1)
     ]
     barrier = pltpu.get_barrier_semaphore()
     for device in partners:
@@ -96,7 +107,7 @@
 
     pl.semaphore_wait(barrier, len(partners))
 
-    pieces_out = [0]
+    rows_out = [0]
     gated_out = [0]
     sent = []
 
@@ -106,25 +117,22 @@
 
     have = {(0, 0, p) for p in range(NP)}
 
+    def rows_of(p):
+        return pl.ds(STARTS[p], PIECES[p])
+
     def piece(item):
         dx, dz, p = item
-        return wbuf.at[chip_block(dx, dz) * 2 + c, pl.ds(p * PIECE, PIECE)]
+        return wbuf.at[chip_block(dx, dz) * 2 + c, rows_of(p)]
 
     def source(item):
-        dx, dz, p = item
-        if (dx % 4, dz) == (0, 0):
-            return w_hbm.at[pl.ds(p * PIECE, PIECE)]
-        assert (dx % 4, dz, p) in have
-        return piece(item)
+        return w_hbm.at[rows_of(item[2])] if item[:2] == (0, 0) else piece(item)
 
     links = (
         (X_RIGHT, r_xr, dict(dx=1), -1, 0),
         (X_LEFT, r_xl, dict(dx=3), 1, 0),
         (Z_SEND, r_z, dict(dzh=1), 0, 1),
     )
-
     issued = [0] * len(links)
-
     limits = [EARLY, EARLY, EARLY]
 
     def issue():
@@ -136,31 +144,44 @@
                     if (dx % 4, dz, p) not in have:
                         break
                     remote(source(items[r]), piece(items[r]), s_w, rsem.at[r], at(**where)).start()
-                    pieces_out[0] += 1
+                    rows_out[0] += PIECES[p]
                 issued[i] += 1
 
-    def absorb(r):
-        for items, rsem, where, ox, oz in links:
-            if r < len(items) and items[r] is not None:
-                dx, dz, p = items[r]
-                item = ((dx + ox) % 4, (dz + oz) % 2, p)
-                assert item not in have
-                have.add(item)
-                ref = piece(item)
-                remote(ref, ref, s_w, rsem.at[r], at(**where)).wait_recv()
-                remote(ref, ref, s_w, r_w.at[group(item)], at(dc=1)).start()
-                pieces_out[0] += 1
+    def absorb(i, r):
+        items, rsem, where, ox, oz = links[i]
+        dx, dz, p = items[r]
+        item = ((dx + ox) % 4, (dz + oz) % 2, p)
+        assert item not in have and r < issued[i]
+        have.add(item)
+        ref = piece(item)
+        remote(ref, ref, s_w, rsem.at[r], at(**where)).wait_recv()
+        remote(ref, ref, s_w, r_w.at[group(item)], at(dc=1)).start()
+        rows_out[0] += PIECES[p]
         issue()
+
+    events = sorted(
+        (time, i, r)
+        for i, link in enumerate(links)
+        for r, time in enumerate(times(link[0]))
+        if link[0][r] is not None
+    )
+    events += [(Y_AT + r + 1.0, 3, r) for r in range(NY)]
+    events += [(Z_EARLY + 2.0 + p, 4, p) for p in range(4)]
+    events.sort()
+
+    def absorb_until(time):
+        while events and events[0][0] <= time and events[0][1] < 3:
+            absorb(*events.pop(0)[1:])
 
     def group(item):
         dx, dz, p = item
-        return dx * 2 + dz + (4 if (dx, dz) == (2, 1) and p >= NP // 2 else 0)
+        return dx * 2 + dz + (4 if (dx, dz) == (2, 1) and p >= HALF_P else 0)
 
     def from_sibling(dx, dz, part=None):
         rows = KROWS if part is None else KROWS // 2
         first = (part or 0) * rows
         ref = wbuf.at[chip_block(dx, dz) * 2 + 1 - c, pl.ds(first, rows)]
-        remote(ref, ref, s_w, r_w.at[group((dx, dz, first // PIECE))], at(dc=1)).wait_recv()
+        remote(ref, ref, s_w, r_w.at[group((dx, dz, (part or 0) * HALF_P))], at(dc=1)).wait_recv()
 
     issue()
     own = wbuf.at[s]
@@ -208,31 +229,40 @@
     half = pl.ds(pl.multiple_of(8 * c, 8), 8)
     lam_h = lam_block[half, :]
     mine, other = e_own[half, :], e_sib[half, :]
+    lam2 = lam_h * lam_h
+    lam4 = lam2 * lam2
     e_chip[...] = jnp.where(c == 0, lam_h * mine + other, lam_h * other + mine)
     later = []
-    for d in range(1, 8):
-        j2 = j + d
-        device = ((j2 % 8) * 2 + c, t)
-        later.append((j2 < 8, remote(e_chip, e_in.at[j], s_st.at[d], r_st.at[j], device)))
+    for d in range(1, 4):
+        later.append((x + d < 4, remote(e_chip, e_in.at[x], s_st.at[d - 1], r_st.at[x], at(dx=d))))
     for ok, copy in later:
         pl.when(ok)(copy.start)
-    limits[:] = [NX, NX, Z_EARLY]
-    absorb(0)
+    start(remote(e_chip, e_zh, s_st.at[3], r_st.at[3], at(dzh=1)))
+    limits[:] = [len(X_RIGHT), len(X_LEFT), Z_STATES]
+    issue()
+    absorb_until(2.0)
+    a_own[...] = jnp.zeros((8, CHAN), F32)
+    for x1 in range(3):
+
+        @pl.when(x1 < x)
+        def _(x1=x1):
+            remote(e_chip, e_in.at[x1], s_st.at[0], r_st.at[x1], at(dx=1)).wait_recv()
+            a_own[...] = lam4 * a_own[...] + e_in[x1]
+
+    pass_a = remote(a_own, a_zh, s_st.at[4], r_st.at[4], at(dzh=1))
+    start(pass_a)
+    limits[2] = Z_EARLY
+    issue()
+    absorb_until(3.0)
+    remote(e_chip, e_zh, s_st.at[3], r_st.at[3], at(dzh=1)).wait_recv()
+    pass_a.wait_recv()
+    s_x = jnp.where(zh == 0, lam2 * a_own[...] + a_zh[...], lam2 * a_zh[...] + a_own[...])
     s_half = s_in.at[half, :]
-    s_half[...] = jnp.zeros((8, CHAN), F32)
-    lam2 = lam_h * lam_h
-    for j1 in range(7):
-
-        @pl.when(j1 < j)
-        def _(j1=j1):
-            remote(e_chip, e_in.at[j1], s_st.at[0], r_st.at[j1], at(dc=1)).wait_recv()
-            s_half[...] = lam2 * s_half[...] + e_in[j1]
-
-    pass_s = remote(s_half, s_half, s_e.at[2], r_e.at[2], at(dc=1))
-    start(pass_s)
+    s_half[...] = jnp.where(zh == 0, s_x, lam2 * s_x + e_zh[...])
+    start(remote(s_half, s_half, s_e.at[2], r_e.at[2], at(dc=1)))
+    absorb_until(4.0)
     pass_s_in = s_in.at[pl.ds(pl.multiple_of(8 - 8 * c, 8), 8), :]
     remote(pass_s_in, pass_s_in, s_e.at[2], r_e.at[2], at(dc=1)).wait_recv()
-    absorb(1)
 
     have_g = set()
 
@@ -307,30 +337,18 @@
             remote(ref, ref, s_g, r_g.at[p], at(dzl=1)).start()
             gated_out[0] += 1
             issue_g()
-            if p == 1:
-                absorb(2)
-
-    limits[2] = NZ
+            absorb_until(4.0 + 0.3 * p)
+
+    limits[2] = len(Z_SEND)
     issue()
-    for r in range(3, G_BASE + NY):
-        absorb(r)
-        rg = r - G_BASE
-        if 0 <= rg < 4:
-            absorb_zl(rg)
-        if 0 <= rg:
-            absorb_g(rg)
-
-    own_in.wait()
-    remote(w_hbm, wbuf.at[s + 1 - 2 * c], s_e.at[1], r_e.at[1], at(dc=1)).wait_recv()
-
-    def multiply(dx, dz, part=None, first=False):
+
+    def multiply(dx, dz, part=None, first=False, last=False):
         b = chip_block(dx, dz)
         rows = KROWS if part is None else KROWS // 2
         at_row = (part or 0) * rows
 
-        @pl.loop(0, CHAN, step=256)
-        def _(n):
-            cols = pl.ds(pl.multiple_of(n, 256), 256)
+        for n in range(0, CHAN, 256):
+            cols = pl.ds(n, 256)
             if part is None:
                 w = wbuf[pl.ds(2 * b, 2), :, cols].reshape(2 * KROWS, 256)
                 total = jnp.dot(gbuf[b], w, preferred_element_type=F32)
@@ -343,7 +361,11 @@
                     )
                     for h in range(2)
                 )
-            acc[:, cols] = total if first else acc[:, cols] + total
+            total = total if first else acc[:, cols] + total
+            if last:
+                out_ref[:, cols] = total.astype(BF16)
+            else:
+                acc[:, cols] = total
 
     done = set()
     blocks = [(0, 0), (1, 0), (3, 0), (0, 1), (1, 1), (3, 1), (2, 0)]
@@ -355,20 +377,32 @@
             multiply(*b, first=not done)
             done.add(b)
 
-    for r in range(G_BASE + NY, NX):
-        work(2)
-        absorb(r)
+    waits = [NY + 4]
+    while events:
+        _, i, r = events.pop(0)
+        if i < 3:
+            absorb(i, r)
+        elif i == 3:
+            absorb_g(r)
+        else:
+            absorb_zl(r)
+        if i >= 3:
+            waits[0] -= 1
+            if not waits[0]:
+                own_in.wait()
+                remote(w_hbm, wbuf.at[s + 1 - 2 * c], s_e.at[1], r_e.at[1], at(dc=1)).wait_recv()
+        if not waits[0] and len(events) > 1:
+            work(1)
     work(8)
     assert len(done) == 7
     for part in range(2):
         from_sibling(2, 1, part)
-        multiply(2, 1, part)
-    out_ref[...] = acc[...].astype(BF16)
+        multiply(2, 1, part, last=part == 1)
 
     for copy in sent:
         copy.wait_send()
-    assert pieces_out[0] * PIECE % KROWS == 0 and gated_out[0] % 4 == 0
-    ref = wbuf.at[pl.ds(0, pieces_out[0] * PIECE // KROWS)]
+    assert rows_out[0] % KROWS == 0 and gated_out[0] % 4 == 0
+    ref = wbuf.at[pl.ds(0, rows_out[0] // KROWS)]
     remote(ref, ref, s_w, r_w.at[0], at(dc=1)).wait_send()
     ref = gbuf.at[pl.ds(0, gated_out[0] // 4)]
     remote(ref, ref, s_g, r_g.at[0], at(dc=1)).wait_send()
@@ -381,7 +415,7 @@
     vm = pltpu.VMEM
     return pl.pallas_call(
         kernel,
-        out_shape=jax.ShapeDtypeStruct((ROWS, CHAN), BF16),
+        out_shape=pltpu.VMEM((ROWS, CHAN), BF16),
         in_specs=[pl.BlockSpec(memory_space=pl.ANY)] * 7,
         out_specs=pl.BlockSpec(memory_space=pltpu.VMEM),
         scratch_shapes=[
@@ -390,10 +424,11 @@
             vm((16, KROWS, CHAN), BF16), vm((8, ROWS, CHAN), BF16), vm((ROWS, CHAN), F32),
             vm((GROUPS, ROWS, LANES), F32), vm((GROUPS, ROWS, LANES), F32),
             vm((MODES, 8, CHAN), F32), vm((MODES, 8, CHAN), F32), vm((MODES, 8, CHAN), F32),
-            vm((MODES, CHAN), F32), vm((MODES, CHAN), F32), vm((8, CHAN), F32), vm((7, 8, CHAN), F32),
+            vm((MODES, CHAN), F32), vm((MODES, CHAN), F32), vm((8, CHAN), F32), vm((3, 8, CHAN), F32),
+            vm((8, CHAN), F32), vm((8, CHAN), F32), vm((8, CHAN), F32),
             vm((MODES, CHAN), F32), vm((MODES, CHAN), F32),
-            dma((6,)), dma, dma((NX,)), dma((NX,)), dma((NZ,)), dma, dma((10,)), dma((NY,)), dma((NY,)), dma, dma((4,)),
-            dma((3,)), dma((3,)), dma((8,)), dma((8,)),
+            dma((6,)), dma, dma((len(X_RIGHT),)), dma((len(X_LEFT),)), dma((len(Z_SEND),)), dma, dma((10,)), dma((NY,)), dma((NY,)), dma, dma((4,)),
+            dma((3,)), dma((3,)), dma((5,)), dma((5,)),
         ],
         compiler_params=pltpu.CompilerParams(
             collective_id=0, has_side_effects=True, vmem_limit_bytes=56 << 20

time: 76 us -> 69.7 us (0.917)
  Pallas kernels: 73.3 us -> 68.8 us
  local copies, waits for them, and re-layouts: 1.87 us -> 0.8 us
    pallas_call x1, Pallas kernels: 73.3 us -> 68.8 us  [body(): pl.pallas_call(kernel, out_shape=pltpu.VMEM((ROWS, CHAN), BF16), in_specs...]
    unnamed x1, local copies, waits for them, and re-layouts: 1.87 us -> 0.8 us
where the time goes in v3:
time: 69.7 us; the launch traced here: 69.6 us
  Pallas kernels  68.8 us (99%)
  local copies, waits for them, and re-layouts  0.8 us (1%)
    pallas_call x1, Pallas kernels, body(): pl.pallas_call(kernel, out_shape=pltpu.VMEM((ROWS, CHAN), BF16), in_specs...  68.8 us

profile of v3, /device:TPU:1, one launch (start us, length us, event | category | flops | bytes accessed | tf_op | source)
XLA Modules:
  0.0 69.6 jit_solution(6860900076281703689)
XLA Ops:
  0.0 68.8 %hyena.1 = bf16[256,1024]{1,0:T(8,128)(2,1)S(1)} custom-call(bf16[256,1024]{1,0:T(8,128)(2,1)} %q_hbm.1, bf16[256,1024]{1,0:T(8,128)(2,1)} %k_hbm.1, bf16[256,1024]{1,0:T(8,128)(2,1)} %v_hbm.1, f32[16,1024]{1,0:T(8,128)} %bitcast.3, f32[16,1024]{1,0:T(8,128)} %bitcast.4, f32[1,1024]{1,0:T(1,128)} %bitcast.5, bf16[512,1024]{1,0:T(8,128)(2,1)} %w_hbm.1), custom_call_target="tpu_custom_call" | custom-call | flops 4294967296 | bytes 4194304 | tf_op jit(solution)/shard_map/hyena/pallas_call | solution.py:416
  68.8 0.8 %copy.9 = bf16[256,1024]{1,0:T(8,128)(2,1)} copy(bf16[256,1024]{1,0:T(8,128)(2,1)S(1)} %hyena.1) | data formatting | bytes 1048576

commit v4 on v3

--- a/solution.py
+++ b/solution.py
@@ -15,49 +15,44 @@
 LANES = 128
 GROUPS = CHAN // LANES
 
-PIECES = (64, 64, 64, 64, 64, 32, 32, 64, 64)
-STARTS = tuple(sum(PIECES[:p]) for p in range(len(PIECES)))
-NP, ZFIRST, HALF_P = len(PIECES), 6, 4
+GRAIN = 16
 UNIT = 64
 
 EARLY = 2
 Z_STATES = 3
-Z_EARLY = 5
-
-OWN = [(0, 0, p) for p in range(NP)]
-X_RIGHT = (
-    OWN
-    + [(0, 1, 0), (0, 1, 1), (0, 1, 2), (-1, 0, 6)]
-    + [(0, 1, 3), (0, 1, 4), (0, 1, 5)]
-    + [(-1, 0, p) for p in (0, 2, 4, 5)]
-    + [(-1, 1, p) for p in (0, 2, 5)]
-)
-X_LEFT = (
-    OWN
-    + [(0, 1, 0), (0, 1, 1), (0, 1, 2), (1, 0, 7), (1, 0, 8)]
-    + [(0, 1, 3), (0, 1, 4), (0, 1, 5)]
-    + [(1, 0, p) for p in (1, 3)]
-    + [(1, 1, p) for p in (1, 3, 4)]
-)
-Z_SEND = (
-    OWN[:Z_EARLY]
-    + [None] * 4
-    + OWN[Z_EARLY:]
-    + [(dx, 0, p) for dx in (-1, 1, 2) for p in (6, 7, 8)]
-)
+Z_EARLY = 4
+
+X_OWN = [(0, 0, 0, 64), (0, 0, 64, 64), (0, 0, 128, 128), (0, 0, 256, 96), (0, 0, 352, 160)]
+X_RIGHT = X_OWN + [
+    (0, 1, 0, 128), (0, 1, 128, 64), (-1, 0, 352, 48), (0, 1, 192, 160),
+    (-1, 0, 0, 128), (-1, 0, 128, 96),
+    (-1, 1, 0, 96), (-1, 1, 256, 64),
+]
+X_LEFT = X_OWN + [
+    (0, 1, 0, 128), (0, 1, 128, 64), (1, 0, 400, 112), (0, 1, 192, 160),
+    (1, 0, 224, 128),
+    (1, 1, 96, 160), (1, 1, 320, 32),
+]
+Z_SEND = [(0, 0, 0, 64), (0, 0, 64, 64), (0, 0, 128, 64), (0, 0, 192, 160)] + [None] * 4 + [
+    (0, 0, 352, 160), (-1, 0, 352, 160), (1, 0, 352, 160), (2, 0, 352, 48), (2, 0, 400, 112),
+]
 
 
 def times(items):
     total, out = 0.0, []
     for item in items:
-        total += 1.0 if item is None else PIECES[item[2]] / UNIT
+        total += 1.0 if item is None else item[3] / UNIT
         out.append(total)
     return out
 
 
+def grains(dx, dz, first, rows):
+    return {(dx % 4, dz % 2, g) for g in range(first // GRAIN, (first + rows) // GRAIN)}
+
+
 GP = 256
-Y_RIGHT = [(0, 0, p) for p in range(4)] + [(0, 1, p) for p in range(4)] + [(-1, 0, 0), (-1, 0, 2), (-1, 1, 0), (-1, 1, 2)]
-Y_LEFT = [(0, 0, p) for p in range(4)] + [(0, 1, p) for p in range(4)] + [(1, 0, 1), (1, 0, 3), (1, 1, 1), (1, 1, 3)]
+Y_RIGHT = [(0, 0, p) for p in range(4)] + [(-1, 0, 0), (-1, 0, 2)] + [(0, 1, p) for p in range(4)] + [(-1, 1, 0), (-1, 1, 2)]
+Y_LEFT = [(0, 0, p) for p in range(4)] + [(1, 0, 1), (1, 0, 3)] + [(0, 1, p) for p in range(4)] + [(1, 1, 1), (1, 1, 3)]
 NY = len(Y_RIGHT)
 Y_AT = 5.3
 
@@ -98,8 +93,8 @@
     ]
     for cp in ins:
         cp.start()
-    partners = [at(dc=1), at(dy=1), at(dy=3), at(dzl=1)] + [
-        at(dx=1), at(dx=2), at(dx=3), at(dzh=1)
+    partners = [
+        at(dzh=1), at(dx=2), at(dx=1), at(dx=3), at(dy=1), at(dy=3), at(dzl=1), at(dc=1)
     ]
     barrier = pltpu.get_barrier_semaphore()
     for device in partners:
@@ -115,17 +110,14 @@
         copy.start()
         sent.append(copy)
 
-    have = {(0, 0, p) for p in range(NP)}
-
-    def rows_of(p):
-        return pl.ds(STARTS[p], PIECES[p])
+    have = grains(0, 0, 0, KROWS)
 
     def piece(item):
-        dx, dz, p = item
-        return wbuf.at[chip_block(dx, dz) * 2 + c, rows_of(p)]
+        dx, dz, first, rows = item
+        return wbuf.at[chip_block(dx, dz) * 2 + c, pl.ds(first, rows)]
 
     def source(item):
-        return w_hbm.at[rows_of(item[2])] if item[:2] == (0, 0) else piece(item)
+        return w_hbm.at[pl.ds(item[2], item[3])] if item[:2] == (0, 0) else piece(item)
 
     links = (
         (X_RIGHT, r_xr, dict(dx=1), -1, 0),
@@ -140,33 +132,32 @@
             while issued[i] < min(limits[i], len(items)):
                 r = issued[i]
                 if items[r] is not None:
-                    dx, dz, p = items[r]
-                    if (dx % 4, dz, p) not in have:
+                    if not grains(*items[r]) <= have:
                         break
                     remote(source(items[r]), piece(items[r]), s_w, rsem.at[r], at(**where)).start()
-                    rows_out[0] += PIECES[p]
+                    rows_out[0] += items[r][3]
                 issued[i] += 1
 
     def absorb(i, r):
         items, rsem, where, ox, oz = links[i]
-        dx, dz, p = items[r]
-        item = ((dx + ox) % 4, (dz + oz) % 2, p)
-        assert item not in have and r < issued[i]
-        have.add(item)
+        dx, dz, first, rows = items[r]
+        item = ((dx + ox) % 4, (dz + oz) % 2, first, rows)
+        assert not grains(*item) & have and r < issued[i]
+        have.update(grains(*item))
         ref = piece(item)
         remote(ref, ref, s_w, rsem.at[r], at(**where)).wait_recv()
         remote(ref, ref, s_w, r_w.at[group(item)], at(dc=1)).start()
-        rows_out[0] += PIECES[p]
+        rows_out[0] += rows
         issue()
 
     events = sorted(
-        (time, i, r)
+        (time + (i == 2) * 0.5, i, r)
         for i, link in enumerate(links)
         for r, time in enumerate(times(link[0]))
         if link[0][r] is not None
     )
     events += [(Y_AT + r + 1.0, 3, r) for r in range(NY)]
-    events += [(Z_EARLY + 2.0 + p, 4, p) for p in range(4)]
+    events += [(times(Z_SEND)[Z_EARLY + p] + 1.0, 4, p) for p in range(4)]
     events.sort()
 
     def absorb_until(time):
@@ -174,14 +165,17 @@
             absorb(*events.pop(0)[1:])
 
     def group(item):
-        dx, dz, p = item
-        return dx * 2 + dz + (4 if (dx, dz) == (2, 1) and p >= HALF_P else 0)
+        dx, dz, first, rows = item
+        if (dx, dz) != (2, 1):
+            return dx * 2 + dz
+        assert first >= KROWS // 2 or first + rows <= KROWS // 2
+        return 8 + first // (KROWS // 2)
 
     def from_sibling(dx, dz, part=None):
         rows = KROWS if part is None else KROWS // 2
         first = (part or 0) * rows
         ref = wbuf.at[chip_block(dx, dz) * 2 + 1 - c, pl.ds(first, rows)]
-        remote(ref, ref, s_w, r_w.at[group((dx, dz, (part or 0) * HALF_P))], at(dc=1)).wait_recv()
+        remote(ref, ref, s_w, r_w.at[group((dx, dz, first, rows))], at(dc=1)).wait_recv()
 
     issue()
     own = wbuf.at[s]
@@ -305,7 +299,6 @@
         issue_g()
 
     before = jnp.where(c == 0, s_in[...], lam_block[...] * s_in[...] + e_sib[...])
-    e_own_state = before
     row_seg = lax.broadcasted_iota(jnp.int32, (8, LANES), 0).astype(F32)
     for g in range(GROUPS):
         lanes = pl.ds(g * LANES, LANES)
@@ -318,7 +311,7 @@
         lift = lift * jnp.where((seg_at // 2) % 2 == 1, power, 1.0)
         power = power * power
         lift = lift * jnp.where(seg_at // 4 == 1, power, 1.0)
-        first = jnp.stack([jnp.broadcast_to(e_own_state[m : m + 1, g * LANES : (g + 1) * LANES], (8, LANES)) for m in range(MODES)])
+        first = jnp.stack([jnp.broadcast_to(before[m : m + 1, g * LANES : (g + 1) * LANES], (8, LANES)) for m in range(MODES)])
         gain = skip[:, lanes]
 
         def step(i, state):
@@ -371,7 +364,7 @@
     blocks = [(0, 0), (1, 0), (3, 0), (0, 1), (1, 1), (3, 1), (2, 0)]
 
     def work(most):
-        for b in [b for b in blocks if b not in done and all((*b, p) in have for p in range(NP))][:most]:
+        for b in [b for b in blocks if b not in done and grains(*b, 0, KROWS) <= have][:most]:
             if b != (0, 0):
                 from_sibling(*b)
             multiply(*b, first=not done)
@@ -391,7 +384,7 @@
             if not waits[0]:
                 own_in.wait()
                 remote(w_hbm, wbuf.at[s + 1 - 2 * c], s_e.at[1], r_e.at[1], at(dc=1)).wait_recv()
-        if not waits[0] and len(events) > 1:
+        if not waits[0] and len(events) > 2:
             work(1)
     work(8)
     assert len(done) == 7
@@ -424,7 +417,7 @@
             vm((16, KROWS, CHAN), BF16), vm((8, ROWS, CHAN), BF16), vm((ROWS, CHAN), F32),
             vm((GROUPS, ROWS, LANES), F32), vm((GROUPS, ROWS, LANES), F32),
             vm((MODES, 8, CHAN), F32), vm((MODES, 8, CHAN), F32), vm((MODES, 8, CHAN), F32),
-            vm((MODES, CHAN), F32), vm((MODES, CHAN), F32), vm((8, CHAN), F32), vm((3, 8, CHAN), F32),
+            vm((MODES, CHAN), F32), vm((MODES, CHAN), F32), vm((8, CHAN), F32), vm((4, 8, CHAN), F32),
             vm((8, CHAN), F32), vm((8, CHAN), F32), vm((8, CHAN), F32),
             vm((MODES, CHAN), F32), vm((MODES, CHAN), F32),
             dma((6,)), dma, dma((len(X_RIGHT),)), dma((len(X_LEFT),)), dma((len(Z_SEND),)), dma, dma((10,)), dma((NY,)), dma((NY,)), dma, dma((4,)),

time: 69.7 us -> 68.8 us (0.987)
  Pallas kernels: 68.8 us -> 67.9 us
    pallas_call x1, Pallas kernels: 68.8 us -> 67.9 us  [body(): pl.pallas_call(kernel, out_shape=pltpu.VMEM((ROWS, CHAN), BF16), in_specs...]
where the time goes in v4:
time: 68.8 us; the launch traced here: 68.7 us
  Pallas kernels  67.9 us (99%)
  local copies, waits for them, and re-layouts  0.8 us (1%)
    pallas_call x1, Pallas kernels, body(): pl.pallas_call(kernel, out_shape=pltpu.VMEM((ROWS, CHAN), BF16), in_specs...  67.9 us

profile of v4, /device:TPU:1, one launch (start us, length us, event | category | flops | bytes accessed | tf_op | source)
XLA Modules:
  0.0 68.7 jit_solution(9918123301833858045)
XLA Ops:
  0.0 67.9 %hyena.1 = bf16[256,1024]{1,0:T(8,128)(2,1)S(1)} custom-call(bf16[256,1024]{1,0:T(8,128)(2,1)} %q_hbm.1, bf16[256,1024]{1,0:T(8,128)(2,1)} %k_hbm.1, bf16[256,1024]{1,0:T(8,128)(2,1)} %v_hbm.1, f32[16,1024]{1,0:T(8,128)} %bitcast.3, f32[16,1024]{1,0:T(8,128)} %bitcast.4, f32[1,1024]{1,0:T(1,128)} %bitcast.5, bf16[512,1024]{1,0:T(8,128)(2,1)} %w_hbm.1), custom_call_target="tpu_custom_call" | custom-call | flops 4294967296 | bytes 4194304 | tf_op jit(solution)/shard_map/hyena/pallas_call | solution.py:409
  67.9 0.8 %copy.9 = bf16[256,1024]{1,0:T(8,128)(2,1)} copy(bf16[256,1024]{1,0:T(8,128)(2,1)S(1)} %hyena.1) | data formatting | bytes 1048576

commit v5 on v4

--- a/solution.py
+++ b/solution.py
@@ -335,26 +335,21 @@
     limits[2] = len(Z_SEND)
     issue()
 
-    def multiply(dx, dz, part=None, first=False, last=False):
+    def multiply(dx, dz, first=False):
         b = chip_block(dx, dz)
-        rows = KROWS if part is None else KROWS // 2
-        at_row = (part or 0) * rows
-
         for n in range(0, CHAN, 256):
             cols = pl.ds(n, 256)
-            if part is None:
-                w = wbuf[pl.ds(2 * b, 2), :, cols].reshape(2 * KROWS, 256)
-                total = jnp.dot(gbuf[b], w, preferred_element_type=F32)
-            else:
-                total = sum(
-                    jnp.dot(
-                        gbuf[b, :, pl.ds(h * KROWS + at_row, rows)],
-                        wbuf[2 * b + h, pl.ds(at_row, rows), cols],
-                        preferred_element_type=F32,
-                    )
-                    for h in range(2)
-                )
-            total = total if first else acc[:, cols] + total
+            w = wbuf[pl.ds(2 * b, 2), :, cols].reshape(2 * KROWS, 256)
+            total = jnp.dot(gbuf[b], w, preferred_element_type=F32)
+            acc[:, cols] = total if first else acc[:, cols] + total
+
+    def multiply_rows(dx, dz, core, first, rows, last=False):
+        b = chip_block(dx, dz)
+        depth = pl.ds(pl.multiple_of(core * KROWS + first, 256), rows)
+        for n in range(0, CHAN, 256):
+            cols = pl.ds(n, 256)
+            w = wbuf[2 * b + core, pl.ds(first, rows), cols]
+            total = acc[:, cols] + jnp.dot(gbuf[b, :, depth], w, preferred_element_type=F32)
             if last:
                 out_ref[:, cols] = total.astype(BF16)
             else:
@@ -388,9 +383,10 @@
             work(1)
     work(8)
     assert len(done) == 7
+    multiply_rows(2, 1, c, 0, KROWS)
     for part in range(2):
         from_sibling(2, 1, part)
-        multiply(2, 1, part, last=part == 1)
+        multiply_rows(2, 1, 1 - c, part * KROWS // 2, KROWS // 2, last=part == 1)
 
     for copy in sent:
         copy.wait_send()

time: 68.8 us -> 68.7 us (level)
  no operation moved by 1% of the time
where the time goes in v5:
time: 68.7 us; the launch traced here: 68.6 us
  Pallas kernels  67.8 us (99%)
  local copies, waits for them, and re-layouts  0.8 us (1%)
    pallas_call x1, Pallas kernels, body(): pl.pallas_call(kernel, out_shape=pltpu.VMEM((ROWS, CHAN), BF16), in_specs...  67.8 us

profile of v5, /device:TPU:1, one launch (start us, length us, event | category | flops | bytes accessed | tf_op | source)
XLA Modules:
  0.0 68.6 jit_solution(8354459236704768683)
XLA Ops:
  0.0 67.8 %hyena.1 = bf16[256,1024]{1,0:T(8,128)(2,1)S(1)} custom-call(bf16[256,1024]{1,0:T(8,128)(2,1)} %q_hbm.1, bf16[256,1024]{1,0:T(8,128)(2,1)} %k_hbm.1, bf16[256,1024]{1,0:T(8,128)(2,1)} %v_hbm.1, f32[16,1024]{1,0:T(8,128)} %bitcast.3, f32[16,1024]{1,0:T(8,128)} %bitcast.4, f32[1,1024]{1,0:T(1,128)} %bitcast.5, bf16[512,1024]{1,0:T(8,128)(2,1)} %w_hbm.1), custom_call_target="tpu_custom_call" | custom-call | flops 4294967296 | bytes 4194304 | tf_op jit(solution)/shard_map/hyena/pallas_call | solution.py:405
  67.8 0.8 %copy.9 = bf16[256,1024]{1,0:T(8,128)(2,1)} copy(bf16[256,1024]{1,0:T(8,128)(2,1)S(1)} %hyena.1) | data formatting | bytes 1048576
